TPU v7x, 32 devices: a whole 2x2x4 slice. The times are simulated.
32 devices in a mesh: parts: 2 (over y), wide: 8 (over z, core), tp: 2 (over x), sub: 1.
Axes of the slice: x: 2, y: 2, z: 4, core: 2. Of those that a mesh axis runs over, the one named last changes fastest.
Arguments:
- queries: bfloat16 [4096, 8192], P(('parts', 'wide'), ('tp', 'sub')), parts along dimension 0, may hold values from -130 to 130
- resp_kv: bfloat16 [4096, 2048], P(('parts', 'wide'), ('tp', 'sub')), parts along dimension 0, may hold values from -6 to 6
- prefix_pool: bfloat16 [16384, 2048], P(('parts', 'wide'), ('tp', 'sub')), parts along dimension 0, may hold values from -6 to 6
- out_weight: bfloat16 [8192, 5120], P(('tp', 'sub')), may hold values from -0.375 to 0.375
- pre_len: int32 [8], P('parts'), parts along dimension 0, may hold values from 1 to 16, 40 in all
- prompt_blocks: int32 [8], P('parts'), parts along dimension 0, may hold values from 1 to 5, 12 in all
- prompt_owner: int32 [8], P('parts'), parts along dimension 0, may hold values from 0 to 7
- resp_seg: int32 [32], P(('parts', 'wide')), parts along dimension 0, may hold values from 0 to 15, as said below
Outputs:
- scored: bfloat16 [4096, 5120], P(('parts', 'wide'), ('tp', 'sub')), parts along dimension 0
There are 2 independent parts, one for each index of `parts`. A program takes and returns all parts, laid end to end along the dimension named above; an argument that names none is the same for every part. Nothing has to cross between parts.
Inputs may be any that keep to these rules, and one draw needn't show every extreme that they name: prompt_blocks sums to 2 * (8 - 4) + 4. resp_seg never falls along the blocks, and blocks with equal resp_seg lie in one aligned group of 2 blocks.
All inputs are finite; a program needn't handle non-finite values.
Results may differ from a plain program's by a relative error of at most 0.02.
Values may be sent and summed in bfloat16 or wider, within the bound.
No kernel may reach another device: no remote copies, remote signals or barrier semaphores. Data moves between devices by JAX's collectives and lax.ppermute only.
A program may use at most 192 MiB of HBM per device.

v0:
```python
import math

import jax
import jax.numpy as jnp
from jax import lax
from jax.sharding import PartitionSpec as P

HD = 128
BLOCK = 128
RB_DEV = 2
PROMPTS = 4
PMAX = 16
GROUP = 8


NEG_LARGE = -1e30


def table_lookup(indices, values):
    matches = indices[..., None] == jnp.arange(values.shape[0], dtype=jnp.int32)
    return jnp.sum(jnp.where(matches, values, 0), axis=-1)


def block_prompts(first_block, block_count, prompt_blocks):
    block_ends = jnp.cumsum(prompt_blocks + (RB_DEV - 1))
    blocks = first_block + jnp.arange(block_count, dtype=jnp.int32)
    return jnp.sum((blocks[:, None] >= block_ends[None, :]).astype(jnp.int32), axis=1)


def absorb(carried, keys_values, visible, grouped):
    running_max, running_sum, weighted = carried
    kv_heads = keys_values.shape[1] // (2 * HD)
    halves = keys_values.reshape(keys_values.shape[0], kv_heads, 2, HD)
    scores = jnp.einsum(
        "tgeh,kgh->tgek", grouped, halves[:, :, 0], preferred_element_type=jnp.float32
    ) * (1.0 / math.sqrt(HD))
    shown = visible[:, None, None, :]
    scores = jnp.where(shown, scores, NEG_LARGE)
    new_max = jnp.maximum(running_max, jnp.max(scores, axis=-1))
    weights = jnp.where(shown, jnp.exp(scores - new_max[..., None]), 0.0)
    rescale = jnp.exp(running_max - new_max)
    running_sum = running_sum * rescale + jnp.sum(weights, axis=-1)
    weighted = weighted * rescale[..., None] + jnp.einsum(
        "tgek,kgh->tgeh",
        weights.astype(jnp.bfloat16),
        halves[:, :, 1],
        preferred_element_type=jnp.float32,
    )
    return (new_max, running_sum, weighted)


def sweep(carried, rows_kv, describe, tok_prompt, grouped):
    row_count = rows_kv.shape[0]
    span_rows = math.gcd(row_count, 512)
    stacked = rows_kv.reshape(row_count // span_rows, span_rows, rows_kv.shape[1])
    offsets = jnp.arange(row_count // span_rows, dtype=jnp.int32) * span_rows

    def one_block(running, element):
        block_kv, offset = element
        row_ids = offset + jnp.arange(span_rows, dtype=jnp.int32)
        key_prompt, key_usable = describe(row_ids)
        visible = (key_prompt[None, :] == tok_prompt[:, None]) & key_usable[None, :]
        return (absorb(running, block_kv, visible, grouped), None)

    return lax.scan(one_block, carried, (stacked, offsets))[0]


def pool_layout(row_ids, owners, prefix_len, wide_count, stride):
    page_ids = row_ids // BLOCK
    per_owner = PROMPTS * stride
    owner_dev = page_ids // per_owner
    within = page_ids % per_owner
    prompt = within // stride
    position = (
        within % stride * wide_count + (owner_dev - table_lookup(prompt, owners)) % wide_count
    )
    return (prompt, position < table_lookup(prompt, prefix_len))


def local(
    queries, resp_kv, prefix_pool, out_weight, pre_len, prompt_blocks, prompt_owner, resp_seg
):
    wide_count = lax.axis_size("wide")
    device_index = lax.axis_index("wide")
    stride = (PMAX + wide_count - 1) // wide_count
    tok_count = queries.shape[0]
    kv_heads = resp_kv.shape[1] // (2 * HD)
    grouped = queries.reshape(tok_count, kv_heads, GROUP, HD)
    own_prompts = block_prompts(device_index * RB_DEV, RB_DEV, prompt_blocks)
    tok_prompt = jnp.broadcast_to(own_prompts[:, None], (RB_DEV, BLOCK)).reshape(tok_count)
    tok_seg = jnp.broadcast_to(resp_seg[:, None], (RB_DEV, BLOCK)).reshape(tok_count)
    initial = (
        jnp.full((tok_count, kv_heads, GROUP), NEG_LARGE, jnp.float32),
        jnp.zeros((tok_count, kv_heads, GROUP), jnp.float32),
        jnp.zeros((tok_count, kv_heads, GROUP, HD), jnp.float32),
    )

    def describe_pool(row_ids):
        return pool_layout(row_ids, prompt_owner, pre_len, wide_count, stride)

    carried = sweep(
        initial,
        lax.all_gather(prefix_pool, "wide", axis=0, tiled=True),
        describe_pool,
        tok_prompt,
        grouped,
    )
    positions = jnp.arange(tok_count, dtype=jnp.int32)
    same_response = (
        (tok_seg[:, None] == tok_seg[None, :])
        & (tok_prompt[:, None] == tok_prompt[None, :])
        & (positions[None, :] <= positions[:, None])
    )
    running_max, running_sum, weighted = absorb(carried, resp_kv, same_response, grouped)
    attended = (
        (weighted / running_sum[..., None])
        .astype(jnp.bfloat16)
        .reshape(tok_count, kv_heads * GROUP * HD)
    )
    head_terms = jnp.dot(attended, out_weight, preferred_element_type=jnp.float32)
    return lax.psum_scatter(
        head_terms.astype(jnp.bfloat16), ("tp", "sub"), scatter_dimension=1, tiled=True
    )


def solution(mesh):
    return jax.shard_map(
        local,
        mesh=mesh,
        in_specs=(
            P(("parts", "wide"), ("tp", "sub")),
            P(("parts", "wide"), ("tp", "sub")),
            P(("parts", "wide"), ("tp", "sub")),
            P(("tp", "sub"), None),
            P("parts"),
            P("parts"),
            P("parts"),
            P(("parts", "wide")),
        ),
        out_specs=P(("parts", "wide"), ("tp", "sub")),
        check_vma=False,
    )
```

profile of v0, /device:TPU:0, one launch (start us, length us, event | category | flops | bytes accessed | tf_op | source)
XLA Modules:
  0.0 740.7 jit_solution(6494854549482189401)
XLA Ops:
  22.5 140.3 %all-gather.2.cloned.1.call-done = bf16[8192,1024]{1,0:T(8,128)(2,1)} async-done(((bf16[1024,1024]{1,0:T(8,128)(2,1)}), bf16[8192,1024]{1,0:T(8,128)(2,1)}) %all-gather.2.cloned.1.call-update) | async-done | bytes 16777232 | tf_op jit(solution)/shard_map/all_gather | solution.py:103
  162.8 505.0 %while.18 = (s32[]{:T(128)}, f32[256,4,8]{0,2,1:T(8,128)S(1)}, f32[256,4,8]{0,2,1:T(8,128)S(1)}, f32[256,4,8,128]{0,3,2,1:T(8,128)}, s32[16]{0:T(128)S(1)}, /*in...) while((s32[]{:T(128)}, f32[256,4,8]{0,2,1:T(8,128)S(1)}, ...), condition=%wide.region_7.8_spmd.clone, body=%wide.region_2.7_spmd.clone.sunk | while | flops 2205520384 | bytes 138429712 | solution.py:65
  167.7 8.4 %fusion.58 = (f32[256,4,8]{0,2,1:T(8,128)S(1)}, f32[4,512,256,8]{2,1,3,0:T(8,128)}) fusion(pred[256,512]{0,1:T(8,128)(4,1)S(1)} %compare_and_fusion.2, bf16[256,4,8,128]{3,0,2,1:T(8,128)(2,1)S(1)} %get-tuple-element.384, bf16[512,4,2,128]{0,3,2,1:T(8,128)(2,1)} %bitcast.107), kind=kOutput, calls=%fused_computation.3.clone.1 | convolution fusion | flops 1086316544 | bytes 19562496 | tf_op jit(solution)/shard_map/while/body/eval_jaxpr/tgeh,kgh->tgek/dot_general | solution.py:34
  176.1 8.3 %fusion.59 = f32[256,4,8]{0,2,1:T(8,128)S(1)} fusion(f32[4,512,256,8]{2,1,3,0:T(8,128)} %get-tuple-element.349, f32[256,4,8]{0,2,1:T(8,128)S(1)} %select_maximum_fusion.2, pred[256,512]{0,1:T(8,128)(4,1)S(1)} %compare_and_fusion.2), kind=kLoop, calls=%fused_computation.5.clone.1 | loop fusion | flops 20963328 | bytes 16973824 | tf_op jit(solution)/shard_map/while/body/eval_jaxpr/reduce_sum | solution.py:42
  197.8 8.4 %fusion.58 = (f32[256,4,8]{0,2,1:T(8,128)S(1)}, f32[4,512,256,8]{2,1,3,0:T(8,128)}) fusion(pred[256,512]{0,1:T(8,128)(4,1)S(1)} %compare_and_fusion.2, bf16[256,4,8,128]{3,0,2,1:T(8,128)(2,1)S(1)} %get-tuple-element.384, bf16[512,4,2,128]{0,3,2,1:T(8,128)(2,1)} %bitcast.107), kind=kOutput, calls=%fused_computation.3.clone.1 | convolution fusion | flops 1086316544 | bytes 19562496 | tf_op jit(solution)/shard_map/while/body/eval_jaxpr/tgeh,kgh->tgek/dot_general | solution.py:34
  206.2 8.3 %fusion.59 = f32[256,4,8]{0,2,1:T(8,128)S(1)} fusion(f32[4,512,256,8]{2,1,3,0:T(8,128)} %get-tuple-element.349, f32[256,4,8]{0,2,1:T(8,128)S(1)} %select_maximum_fusion.2, pred[256,512]{0,1:T(8,128)(4,1)S(1)} %compare_and_fusion.2), kind=kLoop, calls=%fused_computation.5.clone.1 | loop fusion | flops 20963328 | bytes 16973824 | tf_op jit(solution)/shard_map/while/body/eval_jaxpr/reduce_sum | solution.py:42
  229.5 8.4 %fusion.58 = (f32[256,4,8]{0,2,1:T(8,128)S(1)}, f32[4,512,256,8]{2,1,3,0:T(8,128)}) fusion(pred[256,512]{0,1:T(8,128)(4,1)S(1)} %compare_and_fusion.2, bf16[256,4,8,128]{3,0,2,1:T(8,128)(2,1)S(1)} %get-tuple-element.384, bf16[512,4,2,128]{0,3,2,1:T(8,128)(2,1)} %bitcast.107), kind=kOutput, calls=%fused_computation.3.clone.1 | convolution fusion | flops 1086316544 | bytes 19562496 | tf_op jit(solution)/shard_map/while/body/eval_jaxpr/tgeh,kgh->tgek/dot_general | solution.py:34
  237.9 8.3 %fusion.59 = f32[256,4,8]{0,2,1:T(8,128)S(1)} fusion(f32[4,512,256,8]{2,1,3,0:T(8,128)} %get-tuple-element.349, f32[256,4,8]{0,2,1:T(8,128)S(1)} %select_maximum_fusion.2, pred[256,512]{0,1:T(8,128)(4,1)S(1)} %compare_and_fusion.2), kind=kLoop, calls=%fused_computation.5.clone.1 | loop fusion | flops 20963328 | bytes 16973824 | tf_op jit(solution)/shard_map/while/body/eval_jaxpr/reduce_sum | solution.py:42
  261.1 8.4 %fusion.58 = (f32[256,4,8]{0,2,1:T(8,128)S(1)}, f32[4,512,256,8]{2,1,3,0:T(8,128)}) fusion(pred[256,512]{0,1:T(8,128)(4,1)S(1)} %compare_and_fusion.2, bf16[256,4,8,128]{3,0,2,1:T(8,128)(2,1)S(1)} %get-tuple-element.384, bf16[512,4,2,128]{0,3,2,1:T(8,128)(2,1)} %bitcast.107), kind=kOutput, calls=%fused_computation.3.clone.1 | convolution fusion | flops 1086316544 | bytes 19562496 | tf_op jit(solution)/shard_map/while/body/eval_jaxpr/tgeh,kgh->tgek/dot_general | solution.py:34
  269.5 8.3 %fusion.59 = f32[256,4,8]{0,2,1:T(8,128)S(1)} fusion(f32[4,512,256,8]{2,1,3,0:T(8,128)} %get-tuple-element.349, f32[256,4,8]{0,2,1:T(8,128)S(1)} %select_maximum_fusion.2, pred[256,512]{0,1:T(8,128)(4,1)S(1)} %compare_and_fusion.2), kind=kLoop, calls=%fused_computation.5.clone.1 | loop fusion | flops 20963328 | bytes 16973824 | tf_op jit(solution)/shard_map/while/body/eval_jaxpr/reduce_sum | solution.py:42
  292.8 8.4 %fusion.58 = (f32[256,4,8]{0,2,1:T(8,128)S(1)}, f32[4,512,256,8]{2,1,3,0:T(8,128)}) fusion(pred[256,512]{0,1:T(8,128)(4,1)S(1)} %compare_and_fusion.2, bf16[256,4,8,128]{3,0,2,1:T(8,128)(2,1)S(1)} %get-tuple-element.384, bf16[512,4,2,128]{0,3,2,1:T(8,128)(2,1)} %bitcast.107), kind=kOutput, calls=%fused_computation.3.clone.1 | convolution fusion | flops 1086316544 | bytes 19562496 | tf_op jit(solution)/shard_map/while/body/eval_jaxpr/tgeh,kgh->tgek/dot_general | solution.py:34
  301.2 8.3 %fusion.59 = f32[256,4,8]{0,2,1:T(8,128)S(1)} fusion(f32[4,512,256,8]{2,1,3,0:T(8,128)} %get-tuple-element.349, f32[256,4,8]{0,2,1:T(8,128)S(1)} %select_maximum_fusion.2, pred[256,512]{0,1:T(8,128)(4,1)S(1)} %compare_and_fusion.2), kind=kLoop, calls=%fused_computation.5.clone.1 | loop fusion | flops 20963328 | bytes 16973824 | tf_op jit(solution)/shard_map/while/body/eval_jaxpr/reduce_sum | solution.py:42
  324.5 8.4 %fusion.58 = (f32[256,4,8]{0,2,1:T(8,128)S(1)}, f32[4,512,256,8]{2,1,3,0:T(8,128)}) fusion(pred[256,512]{0,1:T(8,128)(4,1)S(1)} %compare_and_fusion.2, bf16[256,4,8,128]{3,0,2,1:T(8,128)(2,1)S(1)} %get-tuple-element.384, bf16[512,4,2,128]{0,3,2,1:T(8,128)(2,1)} %bitcast.107), kind=kOutput, calls=%fused_computation.3.clone.1 | convolution fusion | flops 1086316544 | bytes 19562496 | tf_op jit(solution)/shard_map/while/body/eval_jaxpr/tgeh,kgh->tgek/dot_general | solution.py:34
  332.9 8.3 %fusion.59 = f32[256,4,8]{0,2,1:T(8,128)S(1)} fusion(f32[4,512,256,8]{2,1,3,0:T(8,128)} %get-tuple-element.349, f32[256,4,8]{0,2,1:T(8,128)S(1)} %select_maximum_fusion.2, pred[256,512]{0,1:T(8,128)(4,1)S(1)} %compare_and_fusion.2), kind=kLoop, calls=%fused_computation.5.clone.1 | loop fusion | flops 20963328 | bytes 16973824 | tf_op jit(solution)/shard_map/while/body/eval_jaxpr/reduce_sum | solution.py:42
  356.1 8.4 %fusion.58 = (f32[256,4,8]{0,2,1:T(8,128)S(1)}, f32[4,512,256,8]{2,1,3,0:T(8,128)}) fusion(pred[256,512]{0,1:T(8,128)(4,1)S(1)} %compare_and_fusion.2, bf16[256,4,8,128]{3,0,2,1:T(8,128)(2,1)S(1)} %get-tuple-element.384, bf16[512,4,2,128]{0,3,2,1:T(8,128)(2,1)} %bitcast.107), kind=kOutput, calls=%fused_computation.3.clone.1 | convolution fusion | flops 1086316544 | bytes 19562496 | tf_op jit(solution)/shard_map/while/body/eval_jaxpr/tgeh,kgh->tgek/dot_general | solution.py:34
  364.5 8.3 %fusion.59 = f32[256,4,8]{0,2,1:T(8,128)S(1)} fusion(f32[4,512,256,8]{2,1,3,0:T(8,128)} %get-tuple-element.349, f32[256,4,8]{0,2,1:T(8,128)S(1)} %select_maximum_fusion.2, pred[256,512]{0,1:T(8,128)(4,1)S(1)} %compare_and_fusion.2), kind=kLoop, calls=%fused_computation.5.clone.1 | loop fusion | flops 20963328 | bytes 16973824 | tf_op jit(solution)/shard_map/while/body/eval_jaxpr/reduce_sum | solution.py:42
  387.8 8.4 %fusion.58 = (f32[256,4,8]{0,2,1:T(8,128)S(1)}, f32[4,512,256,8]{2,1,3,0:T(8,128)}) fusion(pred[256,512]{0,1:T(8,128)(4,1)S(1)} %compare_and_fusion.2, bf16[256,4,8,128]{3,0,2,1:T(8,128)(2,1)S(1)} %get-tuple-element.384, bf16[512,4,2,128]{0,3,2,1:T(8,128)(2,1)} %bitcast.107), kind=kOutput, calls=%fused_computation.3.clone.1 | convolution fusion | flops 1086316544 | bytes 19562496 | tf_op jit(solution)/shard_map/while/body/eval_jaxpr/tgeh,kgh->tgek/dot_general | solution.py:34
  396.2 8.3 %fusion.59 = f32[256,4,8]{0,2,1:T(8,128)S(1)} fusion(f32[4,512,256,8]{2,1,3,0:T(8,128)} %get-tuple-element.349, f32[256,4,8]{0,2,1:T(8,128)S(1)} %select_maximum_fusion.2, pred[256,512]{0,1:T(8,128)(4,1)S(1)} %compare_and_fusion.2), kind=kLoop, calls=%fused_computation.5.clone.1 | loop fusion | flops 20963328 | bytes 16973824 | tf_op jit(solution)/shard_map/while/body/eval_jaxpr/reduce_sum | solution.py:42
  419.4 8.4 %fusion.58 = (f32[256,4,8]{0,2,1:T(8,128)S(1)}, f32[4,512,256,8]{2,1,3,0:T(8,128)}) fusion(pred[256,512]{0,1:T(8,128)(4,1)S(1)} %compare_and_fusion.2, bf16[256,4,8,128]{3,0,2,1:T(8,128)(2,1)S(1)} %get-tuple-element.384, bf16[512,4,2,128]{0,3,2,1:T(8,128)(2,1)} %bitcast.107), kind=kOutput, calls=%fused_computation.3.clone.1 | convolution fusion | flops 1086316544 | bytes 19562496 | tf_op jit(solution)/shard_map/while/body/eval_jaxpr/tgeh,kgh->tgek/dot_general | solution.py:34
  427.9 8.3 %fusion.59 = f32[256,4,8]{0,2,1:T(8,128)S(1)} fusion(f32[4,512,256,8]{2,1,3,0:T(8,128)} %get-tuple-element.349, f32[256,4,8]{0,2,1:T(8,128)S(1)} %select_maximum_fusion.2, pred[256,512]{0,1:T(8,128)(4,1)S(1)} %compare_and_fusion.2), kind=kLoop, calls=%fused_computation.5.clone.1 | loop fusion | flops 20963328 | bytes 16973824 | tf_op jit(solution)/shard_map/while/body/eval_jaxpr/reduce_sum | solution.py:42
  451.1 8.4 %fusion.58 = (f32[256,4,8]{0,2,1:T(8,128)S(1)}, f32[4,512,256,8]{2,1,3,0:T(8,128)}) fusion(pred[256,512]{0,1:T(8,128)(4,1)S(1)} %compare_and_fusion.2, bf16[256,4,8,128]{3,0,2,1:T(8,128)(2,1)S(1)} %get-tuple-element.384, bf16[512,4,2,128]{0,3,2,1:T(8,128)(2,1)} %bitcast.107), kind=kOutput, calls=%fused_computation.3.clone.1 | convolution fusion | flops 1086316544 | bytes 19562496 | tf_op jit(solution)/shard_map/while/body/eval_jaxpr/tgeh,kgh->tgek/dot_general | solution.py:34
  459.5 8.3 %fusion.59 = f32[256,4,8]{0,2,1:T(8,128)S(1)} fusion(f32[4,512,256,8]{2,1,3,0:T(8,128)} %get-tuple-element.349, f32[256,4,8]{0,2,1:T(8,128)S(1)} %select_maximum_fusion.2, pred[256,512]{0,1:T(8,128)(4,1)S(1)} %compare_and_fusion.2), kind=kLoop, calls=%fused_computation.5.clone.1 | loop fusion | flops 20963328 | bytes 16973824 | tf_op jit(solution)/shard_map/while/body/eval_jaxpr/reduce_sum | solution.py:42
  482.8 8.4 %fusion.58 = (f32[256,4,8]{0,2,1:T(8,128)S(1)}, f32[4,512,256,8]{2,1,3,0:T(8,128)}) fusion(pred[256,512]{0,1:T(8,128)(4,1)S(1)} %compare_and_fusion.2, bf16[256,4,8,128]{3,0,2,1:T(8,128)(2,1)S(1)} %get-tuple-element.384, bf16[512,4,2,128]{0,3,2,1:T(8,128)(2,1)} %bitcast.107), kind=kOutput, calls=%fused_computation.3.clone.1 | convolution fusion | flops 1086316544 | bytes 19562496 | tf_op jit(solution)/shard_map/while/body/eval_jaxpr/tgeh,kgh->tgek/dot_general | solution.py:34
  491.2 8.3 %fusion.59 = f32[256,4,8]{0,2,1:T(8,128)S(1)} fusion(f32[4,512,256,8]{2,1,3,0:T(8,128)} %get-tuple-element.349, f32[256,4,8]{0,2,1:T(8,128)S(1)} %select_maximum_fusion.2, pred[256,512]{0,1:T(8,128)(4,1)S(1)} %compare_and_fusion.2), kind=kLoop, calls=%fused_computation.5.clone.1 | loop fusion | flops 20963328 | bytes 16973824 | tf_op jit(solution)/shard_map/while/body/eval_jaxpr/reduce_sum | solution.py:42
  514.4 8.4 %fusion.58 = (f32[256,4,8]{0,2,1:T(8,128)S(1)}, f32[4,512,256,8]{2,1,3,0:T(8,128)}) fusion(pred[256,512]{0,1:T(8,128)(4,1)S(1)} %compare_and_fusion.2, bf16[256,4,8,128]{3,0,2,1:T(8,128)(2,1)S(1)} %get-tuple-element.384, bf16[512,4,2,128]{0,3,2,1:T(8,128)(2,1)} %bitcast.107), kind=kOutput, calls=%fused_computation.3.clone.1 | convolution fusion | flops 1086316544 | bytes 19562496 | tf_op jit(solution)/shard_map/while/body/eval_jaxpr/tgeh,kgh->tgek/dot_general | solution.py:34
  522.8 8.3 %fusion.59 = f32[256,4,8]{0,2,1:T(8,128)S(1)} fusion(f32[4,512,256,8]{2,1,3,0:T(8,128)} %get-tuple-element.349, f32[256,4,8]{0,2,1:T(8,128)S(1)} %select_maximum_fusion.2, pred[256,512]{0,1:T(8,128)(4,1)S(1)} %compare_and_fusion.2), kind=kLoop, calls=%fused_computation.5.clone.1 | loop fusion | flops 20963328 | bytes 16973824 | tf_op jit(solution)/shard_map/while/body/eval_jaxpr/reduce_sum | solution.py:42
  546.1 8.4 %fusion.58 = (f32[256,4,8]{0,2,1:T(8,128)S(1)}, f32[4,512,256,8]{2,1,3,0:T(8,128)}) fusion(pred[256,512]{0,1:T(8,128)(4,1)S(1)} %compare_and_fusion.2, bf16[256,4,8,128]{3,0,2,1:T(8,128)(2,1)S(1)} %get-tuple-element.384, bf16[512,4,2,128]{0,3,2,1:T(8,128)(2,1)} %bitcast.107), kind=kOutput, calls=%fused_computation.3.clone.1 | convolution fusion | flops 1086316544 | bytes 19562496 | tf_op jit(solution)/shard_map/while/body/eval_jaxpr/tgeh,kgh->tgek/dot_general | solution.py:34
  577.8 8.4 %fusion.58 = (f32[256,4,8]{0,2,1:T(8,128)S(1)}, f32[4,512,256,8]{2,1,3,0:T(8,128)}) fusion(pred[256,512]{0,1:T(8,128)(4,1)S(1)} %compare_and_fusion.2, bf16[256,4,8,128]{3,0,2,1:T(8,128)(2,1)S(1)} %get-tuple-element.384, bf16[512,4,2,128]{0,3,2,1:T(8,128)(2,1)} %bitcast.107), kind=kOutput, calls=%fused_computation.3.clone.1 | convolution fusion | flops 1086316544 | bytes 19562496 | tf_op jit(solution)/shard_map/while/body/eval_jaxpr/tgeh,kgh->tgek/dot_general | solution.py:34
  609.4 8.4 %fusion.58 = (f32[256,4,8]{0,2,1:T(8,128)S(1)}, f32[4,512,256,8]{2,1,3,0:T(8,128)}) fusion(pred[256,512]{0,1:T(8,128)(4,1)S(1)} %compare_and_fusion.2, bf16[256,4,8,128]{3,0,2,1:T(8,128)(2,1)S(1)} %get-tuple-element.384, bf16[512,4,2,128]{0,3,2,1:T(8,128)(2,1)} %bitcast.107), kind=kOutput, calls=%fused_computation.3.clone.1 | convolution fusion | flops 1086316544 | bytes 19562496 | tf_op jit(solution)/shard_map/while/body/eval_jaxpr/tgeh,kgh->tgek/dot_general | solution.py:34
  641.1 8.4 %fusion.58 = (f32[256,4,8]{0,2,1:T(8,128)S(1)}, f32[4,512,256,8]{2,1,3,0:T(8,128)}) fusion(pred[256,512]{0,1:T(8,128)(4,1)S(1)} %compare_and_fusion.2, bf16[256,4,8,128]{3,0,2,1:T(8,128)(2,1)S(1)} %get-tuple-element.384, bf16[512,4,2,128]{0,3,2,1:T(8,128)(2,1)} %bitcast.107), kind=kOutput, calls=%fused_computation.3.clone.1 | convolution fusion | flops 1086316544 | bytes 19562496 | tf_op jit(solution)/shard_map/while/body/eval_jaxpr/tgeh,kgh->tgek/dot_general | solution.py:34
  678.7 19.1 %convolution_convert_fusion = bf16[256,5120]{1,0:T(8,128)(2,1)} fusion(bf16[256,4096]{0,1:T(8,128)(2,1)S(1)} %bitcast.111, bf16[4096,5120]{1,0:T(8,128)(2,1)} %param.13), kind=kOutput, calls=%fused_computation.62 | convolution fusion | flops 10738728960 | bytes 46661632 | tf_op jit(solution)/shard_map/dot_general | solution.py:120
  697.9 36.0 %reduce-scatter.2.cloned.1.call-done = bf16[256,2560]{1,0:T(8,128)(2,1)} async-done(((bf16[256,5120]{1,0:T(8,128)(2,1)}), bf16[256,2560]{1,0:T(8,128)(2,1)}) %reduce-scatter.2.cloned.1.call-update) | async-done | bytes 1310736 | tf_op jit(solution)/shard_map/reduce_scatter | solution.py:121
  (298 shorter events, 296.8 us)
Async XLA Ops:
  6.5 156.3 %all-gather.2.cloned.1.call-start = ((), (), s32[]{:S(2)}) async-start(), calls=%async_computation.1 | async-start | bytes 18874368 | tf_op jit(solution)/shard_map/all_gather | solution.py:103
  7.3 726.6 %reduce-scatter.2.cloned.1.call-start = ((), (), s32[]{:S(2)}) async-start(), calls=%async_computation.2 | async-start | bytes 3932160 | tf_op jit(solution)/shard_map/reduce_scatter | solution.py:121
  11.5 151.3 %copy-start.5 = (s32[4]{0:T(128)S(1)}, s32[4]{0:T(128)}, u32[]{:S(2)}) copy-start(s32[4]{0:T(128)} %param.16) | copy-start | bytes 52
  11.5 151.3 %copy-start.6 = (s32[4]{0:T(128)S(1)}, s32[4]{0:T(128)}, u32[]{:S(2)}) copy-start(s32[4]{0:T(128)} %param.14) | copy-start | bytes 52
  14.9 147.9 %copy-start.2 = (bf16[256,1024]{0,1:T(8,128)(2,1)}, bf16[256,1024]{0,1:T(8,128)(2,1)S(1)}, u32[]{:S(2)}) copy-start(bf16[256,1024]{0,1:T(8,128)(2,1)S(1)} %copy.40) | copy-start | bytes 1572868
  167.7 16.8 %copy-start.1 = (bf16[1,512,1024]{1,2,0:T(8,128)(2,1)S(1)}, bf16[1,512,1024]{1,2,0:T(8,128)(2,1)}, u32[]{:S(2)}) copy-start(bf16[1,512,1024]{1,2,0:T(8,128)(2,1)} %copy.58) | copy-start | bytes 3145732 | tf_op jit(solution)/shard_map/while
  176.1 10.7 %copy-start = (f32[4,512,256,8]{2,1,3,0:T(8,128)S(1)}, f32[4,512,256,8]{2,1,3,0:T(8,128)}, u32[]{:S(2)}) copy-start(f32[4,512,256,8]{2,1,3,0:T(8,128)} %get-tuple-element.349) | copy-start | bytes 50331652 | tf_op jit(solution)/shard_map/while
  197.8 16.8 %copy-start.1 = (bf16[1,512,1024]{1,2,0:T(8,128)(2,1)S(1)}, bf16[1,512,1024]{1,2,0:T(8,128)(2,1)}, u32[]{:S(2)}) copy-start(bf16[1,512,1024]{1,2,0:T(8,128)(2,1)} %copy.58) | copy-start | bytes 3145732 | tf_op jit(solution)/shard_map/while
  206.2 10.7 %copy-start = (f32[4,512,256,8]{2,1,3,0:T(8,128)S(1)}, f32[4,512,256,8]{2,1,3,0:T(8,128)}, u32[]{:S(2)}) copy-start(f32[4,512,256,8]{2,1,3,0:T(8,128)} %get-tuple-element.349) | copy-start | bytes 50331652 | tf_op jit(solution)/shard_map/while
  229.5 16.8 %copy-start.1 = (bf16[1,512,1024]{1,2,0:T(8,128)(2,1)S(1)}, bf16[1,512,1024]{1,2,0:T(8,128)(2,1)}, u32[]{:S(2)}) copy-start(bf16[1,512,1024]{1,2,0:T(8,128)(2,1)} %copy.58) | copy-start | bytes 3145732 | tf_op jit(solution)/shard_map/while
  237.9 10.7 %copy-start = (f32[4,512,256,8]{2,1,3,0:T(8,128)S(1)}, f32[4,512,256,8]{2,1,3,0:T(8,128)}, u32[]{:S(2)}) copy-start(f32[4,512,256,8]{2,1,3,0:T(8,128)} %get-tuple-element.349) | copy-start | bytes 50331652 | tf_op jit(solution)/shard_map/while
  261.1 16.8 %copy-start.1 = (bf16[1,512,1024]{1,2,0:T(8,128)(2,1)S(1)}, bf16[1,512,1024]{1,2,0:T(8,128)(2,1)}, u32[]{:S(2)}) copy-start(bf16[1,512,1024]{1,2,0:T(8,128)(2,1)} %copy.58) | copy-start | bytes 3145732 | tf_op jit(solution)/shard_map/while
  269.5 10.7 %copy-start = (f32[4,512,256,8]{2,1,3,0:T(8,128)S(1)}, f32[4,512,256,8]{2,1,3,0:T(8,128)}, u32[]{:S(2)}) copy-start(f32[4,512,256,8]{2,1,3,0:T(8,128)} %get-tuple-element.349) | copy-start | bytes 50331652 | tf_op jit(solution)/shard_map/while
  292.8 16.8 %copy-start.1 = (bf16[1,512,1024]{1,2,0:T(8,128)(2,1)S(1)}, bf16[1,512,1024]{1,2,0:T(8,128)(2,1)}, u32[]{:S(2)}) copy-start(bf16[1,512,1024]{1,2,0:T(8,128)(2,1)} %copy.58) | copy-start | bytes 3145732 | tf_op jit(solution)/shard_map/while
  301.2 10.7 %copy-start = (f32[4,512,256,8]{2,1,3,0:T(8,128)S(1)}, f32[4,512,256,8]{2,1,3,0:T(8,128)}, u32[]{:S(2)}) copy-start(f32[4,512,256,8]{2,1,3,0:T(8,128)} %get-tuple-element.349) | copy-start | bytes 50331652 | tf_op jit(solution)/shard_map/while
  324.5 16.8 %copy-start.1 = (bf16[1,512,1024]{1,2,0:T(8,128)(2,1)S(1)}, bf16[1,512,1024]{1,2,0:T(8,128)(2,1)}, u32[]{:S(2)}) copy-start(bf16[1,512,1024]{1,2,0:T(8,128)(2,1)} %copy.58) | copy-start | bytes 3145732 | tf_op jit(solution)/shard_map/while
  332.9 10.7 %copy-start = (f32[4,512,256,8]{2,1,3,0:T(8,128)S(1)}, f32[4,512,256,8]{2,1,3,0:T(8,128)}, u32[]{:S(2)}) copy-start(f32[4,512,256,8]{2,1,3,0:T(8,128)} %get-tuple-element.349) | copy-start | bytes 50331652 | tf_op jit(solution)/shard_map/while
  356.1 16.8 %copy-start.1 = (bf16[1,512,1024]{1,2,0:T(8,128)(2,1)S(1)}, bf16[1,512,1024]{1,2,0:T(8,128)(2,1)}, u32[]{:S(2)}) copy-start(bf16[1,512,1024]{1,2,0:T(8,128)(2,1)} %copy.58) | copy-start | bytes 3145732 | tf_op jit(solution)/shard_map/while
  364.5 10.7 %copy-start = (f32[4,512,256,8]{2,1,3,0:T(8,128)S(1)}, f32[4,512,256,8]{2,1,3,0:T(8,128)}, u32[]{:S(2)}) copy-start(f32[4,512,256,8]{2,1,3,0:T(8,128)} %get-tuple-element.349) | copy-start | bytes 50331652 | tf_op jit(solution)/shard_map/while
  387.8 16.8 %copy-start.1 = (bf16[1,512,1024]{1,2,0:T(8,128)(2,1)S(1)}, bf16[1,512,1024]{1,2,0:T(8,128)(2,1)}, u32[]{:S(2)}) copy-start(bf16[1,512,1024]{1,2,0:T(8,128)(2,1)} %copy.58) | copy-start | bytes 3145732 | tf_op jit(solution)/shard_map/while
  396.2 10.7 %copy-start = (f32[4,512,256,8]{2,1,3,0:T(8,128)S(1)}, f32[4,512,256,8]{2,1,3,0:T(8,128)}, u32[]{:S(2)}) copy-start(f32[4,512,256,8]{2,1,3,0:T(8,128)} %get-tuple-element.349) | copy-start | bytes 50331652 | tf_op jit(solution)/shard_map/while
  419.4 16.8 %copy-start.1 = (bf16[1,512,1024]{1,2,0:T(8,128)(2,1)S(1)}, bf16[1,512,1024]{1,2,0:T(8,128)(2,1)}, u32[]{:S(2)}) copy-start(bf16[1,512,1024]{1,2,0:T(8,128)(2,1)} %copy.58) | copy-start | bytes 3145732 | tf_op jit(solution)/shard_map/while
  427.8 10.7 %copy-start = (f32[4,512,256,8]{2,1,3,0:T(8,128)S(1)}, f32[4,512,256,8]{2,1,3,0:T(8,128)}, u32[]{:S(2)}) copy-start(f32[4,512,256,8]{2,1,3,0:T(8,128)} %get-tuple-element.349) | copy-start | bytes 50331652 | tf_op jit(solution)/shard_map/while
  451.1 16.8 %copy-start.1 = (bf16[1,512,1024]{1,2,0:T(8,128)(2,1)S(1)}, bf16[1,512,1024]{1,2,0:T(8,128)(2,1)}, u32[]{:S(2)}) copy-start(bf16[1,512,1024]{1,2,0:T(8,128)(2,1)} %copy.58) | copy-start | bytes 3145732 | tf_op jit(solution)/shard_map/while
  459.5 10.7 %copy-start = (f32[4,512,256,8]{2,1,3,0:T(8,128)S(1)}, f32[4,512,256,8]{2,1,3,0:T(8,128)}, u32[]{:S(2)}) copy-start(f32[4,512,256,8]{2,1,3,0:T(8,128)} %get-tuple-element.349) | copy-start | bytes 50331652 | tf_op jit(solution)/shard_map/while
  482.8 16.8 %copy-start.1 = (bf16[1,512,1024]{1,2,0:T(8,128)(2,1)S(1)}, bf16[1,512,1024]{1,2,0:T(8,128)(2,1)}, u32[]{:S(2)}) copy-start(bf16[1,512,1024]{1,2,0:T(8,128)(2,1)} %copy.58) | copy-start | bytes 3145732 | tf_op jit(solution)/shard_map/while
  491.2 10.7 %copy-start = (f32[4,512,256,8]{2,1,3,0:T(8,128)S(1)}, f32[4,512,256,8]{2,1,3,0:T(8,128)}, u32[]{:S(2)}) copy-start(f32[4,512,256,8]{2,1,3,0:T(8,128)} %get-tuple-element.349) | copy-start | bytes 50331652 | tf_op jit(solution)/shard_map/while
  514.4 16.8 %copy-start.1 = (bf16[1,512,1024]{1,2,0:T(8,128)(2,1)S(1)}, bf16[1,512,1024]{1,2,0:T(8,128)(2,1)}, u32[]{:S(2)}) copy-start(bf16[1,512,1024]{1,2,0:T(8,128)(2,1)} %copy.58) | copy-start | bytes 3145732 | tf_op jit(solution)/shard_map/while
  546.1 16.8 %copy-start.1 = (bf16[1,512,1024]{1,2,0:T(8,128)(2,1)S(1)}, bf16[1,512,1024]{1,2,0:T(8,128)(2,1)}, u32[]{:S(2)}) copy-start(bf16[1,512,1024]{1,2,0:T(8,128)(2,1)} %copy.58) | copy-start | bytes 3145732 | tf_op jit(solution)/shard_map/while
  577.8 16.8 %copy-start.1 = (bf16[1,512,1024]{1,2,0:T(8,128)(2,1)S(1)}, bf16[1,512,1024]{1,2,0:T(8,128)(2,1)}, u32[]{:S(2)}) copy-start(bf16[1,512,1024]{1,2,0:T(8,128)(2,1)} %copy.58) | copy-start | bytes 3145732 | tf_op jit(solution)/shard_map/while
  609.4 16.8 %copy-start.1 = (bf16[1,512,1024]{1,2,0:T(8,128)(2,1)S(1)}, bf16[1,512,1024]{1,2,0:T(8,128)(2,1)}, u32[]{:S(2)}) copy-start(bf16[1,512,1024]{1,2,0:T(8,128)(2,1)} %copy.58) | copy-start | bytes 3145732 | tf_op jit(solution)/shard_map/while
  641.1 16.8 %copy-start.1 = (bf16[1,512,1024]{1,2,0:T(8,128)(2,1)S(1)}, bf16[1,512,1024]{1,2,0:T(8,128)(2,1)}, u32[]{:S(2)}) copy-start(bf16[1,512,1024]{1,2,0:T(8,128)(2,1)} %copy.58) | copy-start | bytes 3145732 | tf_op jit(solution)/shard_map/while
  (10 other events, 87.7 us)
Sparse Core Ops, SparseCore 0:
  9.0 153.7 all-gather.1
  698.0 35.8 reduce-scatter.1
where the time goes:
time: 742 us; the launch traced here: 741 us
  matrix products  287 us (39%)
  waiting for transfers between devices  177 us (24%)
  other arithmetic  165 us (22%)
  local copies, waits for them, and re-layouts  96.8 us (13%)
  between operations  13.5 us (2%)
    dot_general x17, matrix products, absorb(): jnp.einsum('tgeh,kgh->tgek', grouped, halves[:, :, 0], preferred_element_...  141 us
    all_gather x1, waiting for transfers between devices, local(): lax.all_gather(prefix_pool, 'wide', axis=0, tiled=True)  140 us
    reduce_sum x17, other arithmetic, absorb(): running_sum = running_sum * rescale + jnp.sum(weights, axis=-1)  138 us
    dot_general x17, matrix products, absorb(): jnp.einsum('tgek,kgh->tgeh', weights.astype(jnp.bfloat16), halves[:, :, 1...  127 us
    dynamic_slice x48, local copies, waits for them, and re-layouts, sweep(): return lax.scan(one_block, carried, (stacked, offsets))[0]  51.3 us
    while x80, local copies, waits for them, and re-layouts  36.8 us
    reduce_scatter x1, waiting for transfers between devices, local(): lax.psum_scatter(head_terms.astype(jnp.bfloat16), ('tp', 'sub'), scatter_...  36 us
    dot_general x1, matrix products, local(): jnp.dot(attended, out_weight, preferred_element_type=jnp.float32)  19.1 us
  transfers between devices with their start and end apart: 2, of which 2 were waited for; matrix products, arithmetic and copies ran while one was open for 2% of the time, Pallas kernels for 0%

commit v1 on v0

v1 whole, which is shorter than its diff:
```python
import math

import jax
import jax.numpy as jnp
from jax import lax
from jax.experimental import pallas as pl
from jax.experimental.pallas import tpu as pltpu
from jax.sharding import PartitionSpec as P

HD = 128
BLOCK = 128
RB_DEV = 2
PROMPTS = 4
PMAX = 16
GROUP = 8
PAIR = 2 * HD
WIDTH = GROUP * HD
ROWS = 256
SPAN = 4
NEAR = 6
FAR = 4
NEG_LARGE = -1e30
SCALE = math.log2(math.e) / math.sqrt(HD)
VMEM_BYTES = 48 * 1024 * 1024

LEN_AT, BLOCKS_AT, OWNER_AT, SEG_AT, ME_AT = 0, 4, 8, 12, 14


def params():
    return pltpu.CompilerParams(vmem_limit_bytes=VMEM_BYTES)


def as_int(flag):
    return jnp.where(flag, 1, 0)


class Layout:
    def __init__(self, ctrl, wide, cores):
        self.ctrl, self.wide, self.cores = ctrl, wide, cores
        self.stride = (PMAX + wide - 1) // wide
        self.me = ctrl[ME_AT]
        self.z, self.core = self.me // cores, self.me % cores
        ends, total = [], 0
        for p in range(PROMPTS):
            total = total + ctrl[BLOCKS_AT + p] + (RB_DEV - 1)
            ends.append(total)
        self.ends = ends

    def prompt_of(self, block):
        return sum(as_int(block >= end) for end in self.ends[:-1])

    def first_of(self, chip):
        return self.prompt_of(chip * self.cores * RB_DEV)

    def last_of(self, chip):
        return self.prompt_of((chip + 1) * self.cores * RB_DEV - 1)

    def length(self, p):
        return self.ctrl[LEN_AT + p]

    def held_by(self, p, j):
        return lax.rem(self.ctrl[OWNER_AT + p] + j, self.wide)

    def held(self, p, who):
        first = lax.rem(who - self.ctrl[OWNER_AT + p] + self.wide, self.wide)
        return sum(as_int(first + k * self.wide < self.length(p)) for k in range(self.stride))

    def above(self, who, p, top):
        return sum(
            jnp.where((o > p) & (o <= top), self.held(o, who), 0) for o in range(PROMPTS)
        )

    def below(self, who, p, low):
        return sum(
            jnp.where((o < p) & (o >= low), self.held(o, who), 0) for o in range(PROMPTS)
        )

    def near_top(self, chip):
        return jnp.where(chip == 0, self.last_of(1), PROMPTS - 1)

    def near_low(self, chip):
        return jnp.where(chip == 3, self.first_of(2), 0)

    def in_plane(self, p, j):
        who = self.held_by(p, j)
        chip = who // self.cores
        gap = chip - self.z
        k = j // self.wide
        down = self.above(who, p, self.near_top(chip)) + k
        far_down = self.above(who, p, PROMPTS - 1) + k
        up = self.below(who, p, self.near_low(chip)) + k
        far_up = self.below(who, p, 0) + k
        inner = (self.z == 1) | (self.z == 2)
        far = jnp.where(gap < 0, far_down, far_up)
        two = (gap == 2) | (gap == -2)
        three = (gap == 3) | (gap == -3)
        return [
            (gap == 0, 0, p * self.stride + k),
            (gap == -1, 1, down),
            (gap == 1, 2, up),
            (two & inner, 3, far),
            ((two & jnp.logical_not(inner)) | three, 4, far + jnp.where(two, FAR, 0)),
        ]


def page_at(buffers, which, page, column):
    rows = pl.ds(pl.multiple_of(page * BLOCK, BLOCK), BLOCK)
    wide = buffers[which].shape[1] > PAIR
    return buffers[which].at[rows, pl.ds(column if wide else 0, PAIR)]


def start_page(buffers, places, column, target, sem):
    for cond, which, page in places:

        @pl.when(cond)
        def _(which=which, page=page):
            pltpu.make_async_copy(page_at(buffers, which, page, column), target, sem).start()


def wait_page(source, target, sem):
    pltpu.make_async_copy(source.at[pl.ds(0, BLOCK), pl.ds(0, PAIR)], target, sem).wait()


def spot(ref, page):
    return ref.at[pl.ds(pl.multiple_of(page * BLOCK, BLOCK), BLOCK), :]


def send_kernel(wide, cores, column, ctrl, pool, right, left, far, sems):
    lay = Layout(ctrl, wide, cores)
    z, last = lay.z, wide // cores - 1
    plans = []
    for p in range(PROMPTS):
        count = lay.held(p, lay.me)
        for k in range(lay.stride):
            here = k < count
            low, top = lay.first_of(z + 1), lay.near_top(z)
            plans.append(
                (here & (z < last) & (p >= low) & (p <= top), p, k, right, 0, lay.above(lay.me, p, top) + k)
            )
            low, top = lay.near_low(z), lay.last_of(z - 1)
            plans.append(
                (here & (z > 0) & (p >= low) & (p <= top), p, k, left, 1, lay.below(lay.me, p, low) + k)
            )
            low = lay.first_of(2)
            plans.append(
                (here & (z == 0) & (p >= low), p, k, far, 2, lay.above(lay.me, p, PROMPTS - 1) + k)
            )
            top = lay.last_of(1)
            plans.append(
                (here & (z == last) & (p <= top), p, k, far, 2, lay.below(lay.me, p, 0) + k)
            )

    def copy(plan):
        _, p, k, target, lane, rank = plan
        page = p * lay.stride + k
        return pltpu.make_async_copy(
            page_at([pool], 0, page, column), spot(target, rank), sems.at[lane, page]
        )

    for plan in plans:
        pl.when(plan[0])(lambda plan=plan: copy(plan).start())
    for plan in plans:
        pl.when(plan[0])(lambda plan=plan: copy(plan).wait())


def share_kernel(wide, cores, column, ctrl, *refs):
    buffers, out, sems = refs[:5], refs[5], refs[6]
    lay = Layout(ctrl, wide, cores)
    other = lay.z * cores + (cores - 1 - lay.core)
    half = PMAX // cores
    firsts = [lay.prompt_of(other * RB_DEV), lay.prompt_of(other * RB_DEV + 1)]
    moves = []
    for slot in range(RB_DEV):
        p = firsts[slot]
        shift = lax.rem(lay.core - lay.ctrl[OWNER_AT + p] + wide, cores)
        count = (lay.length(p) - shift + cores - 1) // cores
        if slot == 1:
            count = jnp.where(firsts[1] == firsts[0], 0, count)

        def begin(i, carry, slot=slot, p=p, shift=shift):
            start_page(
                buffers,
                lay.in_plane(p, i * cores + shift),
                column,
                spot(out, slot * half + i),
                sems.at[slot * half + i],
            )
            return carry

        lax.fori_loop(0, count, begin, 0)
        moves.append((slot, count))
    for slot, count in moves:

        def finish(i, carry, slot=slot):
            wait_page(buffers[0], spot(out, slot * half + i), sems.at[slot * half + i])
            return carry

        lax.fori_loop(0, count, finish, 0)


def attend_kernel(wide, cores, column, ctrl, queries, own, *refs):
    buffers, out = refs[:-6], refs[-6]
    store, stacked, peak, total, sems = refs[-5:]
    lay = Layout(ctrl, wide, cores)
    prompts = [lay.prompt_of(lay.me * RB_DEV + b) for b in range(RB_DEV)]
    same = prompts[0] == prompts[1]
    half = PMAX // cores

    def places(slot, p, j):
        if len(buffers) == 1:
            page = (lay.held_by(p, j) * PROMPTS + p) * lay.stride + j // wide
            return [(j >= 0, 0, page)]
        mine = lax.rem(lay.held_by(p, j), cores) == lay.core
        spots = [(cond & mine, which, page) for cond, which, page in lay.in_plane(p, j)]
        return spots + [(jnp.logical_not(mine), 5, slot * half + j // cores)]

    counts = []
    for slot in range(RB_DEV):
        count = lay.length(prompts[slot])
        if slot == 1:
            count = jnp.where(same, 0, count)

        def begin(j, carry, slot=slot):
            start_page(
                buffers,
                places(slot, prompts[slot], j),
                column,
                spot(store, slot * PMAX + j),
                sems.at[slot * PMAX + j],
            )
            return carry

        lax.fori_loop(0, count, begin, 0)
        counts.append(count)

    def absorb(keys_values, first, mask=None):
        span = keys_values.shape[0]
        keys = keys_values[:, :HD]
        values = jnp.concatenate(
            [keys_values[:, HD:], jnp.ones((span, HD), jnp.bfloat16)], axis=1
        )
        for r in range(0, GROUP * BLOCK, ROWS):
            rows = pl.ds(r, ROWS)
            scores = lax.dot_general(
                stacked[rows, :], keys, (((1,), (1,)), ((), ())), preferred_element_type=jnp.float32
            )
            if mask is not None:
                scores = jnp.where(mask, scores, NEG_LARGE)
            top = jnp.broadcast_to(jnp.max(scores, axis=1, keepdims=True), (ROWS, HD))
            if not first:
                before = peak[rows, :]
                top = jnp.maximum(before, top)
            spread = jnp.concatenate([top] * (span // HD), axis=1)
            weights = jnp.exp2((scores - spread) * SCALE).astype(jnp.bfloat16)
            blended = jnp.dot(weights, values, preferred_element_type=jnp.float32)
            if not first:
                fade = jnp.exp2((before - top) * SCALE)
                blended = total[rows, :] * jnp.concatenate([fade, fade], axis=1) + blended
            peak[rows, :] = top
            total[rows, :] = blended

    for b in range(RB_DEV):
        for e in range(GROUP):
            stacked[e * BLOCK : (e + 1) * BLOCK, :] = queries[
                b * BLOCK : (b + 1) * BLOCK, e * HD : (e + 1) * HD
            ]
        span = (b + 1) * BLOCK
        row = lax.broadcasted_iota(jnp.int32, (ROWS, span), 0) % BLOCK
        key = lax.broadcasted_iota(jnp.int32, (ROWS, span), 1)
        mask = key <= row + b * BLOCK
        if b == 1:
            joined = same & (lay.ctrl[SEG_AT] == lay.ctrl[SEG_AT + 1])
            mask = mask & (key >= jnp.where(joined, 0, BLOCK))
        absorb(own[0:span, :], True, mask)

        def finish(j, carry, b=b):
            wait_page(buffers[0], spot(store, b * PMAX + j), sems.at[b * PMAX + j])
            return carry

        lax.fori_loop(0, counts[b], finish, 0)
        length = lay.length(prompts[b])
        base = 0 if b == 0 else jnp.where(same, 0, PMAX)

        def tile(page, pages):
            at = pl.multiple_of(page * BLOCK, BLOCK)
            absorb(store[pl.ds(at, pages * BLOCK), :], False)

        def full(i, carry, base=base):
            tile(base + i * SPAN, SPAN)
            return carry

        lax.fori_loop(0, length // SPAN, full, 0)
        left = SPAN // 2
        while left:
            done = length // (2 * left) * (2 * left)
            pl.when(length // left % 2 == 1)(
                lambda left=left, done=done, base=base: tile(base + done, left)
            )
            left //= 2
        for e in range(GROUP):
            rows = slice(e * BLOCK, (e + 1) * BLOCK)
            out[b * BLOCK : (b + 1) * BLOCK, e * HD : (e + 1) * HD] = (
                total[rows, :HD] / total[rows, HD:]
            ).astype(jnp.bfloat16)


def attend(wide, cores, head, ctrl, queries, resp_kv, buffers):
    tokens = queries.shape[0]
    return pl.pallas_call(
        lambda *refs: attend_kernel(wide, cores, head * PAIR, *refs),
        out_shape=jax.ShapeDtypeStruct((tokens, WIDTH), jnp.bfloat16),
        grid_spec=pltpu.PrefetchScalarGridSpec(
            num_scalar_prefetch=1,
            grid=(1,),
            in_specs=[
                pl.BlockSpec((tokens, WIDTH), lambda i, c: (0, head)),
                pl.BlockSpec((tokens, PAIR), lambda i, c: (0, head)),
            ]
            + [pl.BlockSpec(memory_space=pl.ANY)] * len(buffers),
            out_specs=pl.BlockSpec((tokens, WIDTH), lambda i, c: (0, 0)),
            scratch_shapes=[
                pltpu.VMEM((RB_DEV * PMAX * BLOCK, PAIR), jnp.bfloat16),
                pltpu.VMEM((GROUP * BLOCK, HD), jnp.bfloat16),
                pltpu.VMEM((GROUP * BLOCK, HD), jnp.float32),
                pltpu.VMEM((GROUP * BLOCK, 2 * HD), jnp.float32),
                pltpu.SemaphoreType.DMA((RB_DEV * PMAX,)),
            ],
        ),
        compiler_params=params(),
        cost_estimate=pl.CostEstimate(
            flops=2 * 2 * tokens * WIDTH * 18 * BLOCK,
            bytes_accessed=2 * tokens * WIDTH * 2 + PMAX * BLOCK * PAIR * 2,
            transcendentals=tokens * GROUP * 18 * BLOCK,
        ),
        name=f"attend_head_{head}",
    )(ctrl, queries, resp_kv, *buffers)


def pages_shape(count):
    return jax.ShapeDtypeStruct((count * BLOCK, PAIR), jnp.bfloat16)


def pack_send(wide, cores, head, ctrl, pool):
    any_spec = pl.BlockSpec(memory_space=pl.ANY)
    return pl.pallas_call(
        lambda *refs: send_kernel(wide, cores, head * PAIR, *refs),
        out_shape=[pages_shape(NEAR)] * 3,
        grid_spec=pltpu.PrefetchScalarGridSpec(
            num_scalar_prefetch=1,
            grid=(1,),
            in_specs=[any_spec],
            out_specs=[any_spec] * 3,
            scratch_shapes=[pltpu.SemaphoreType.DMA((3, PROMPTS * ((PMAX + wide - 1) // wide)))],
        ),
        compiler_params=params(),
        cost_estimate=pl.CostEstimate(
            flops=0, bytes_accessed=2 * 12 * BLOCK * PAIR * 2, transcendentals=0
        ),
        name=f"pack_send_{head}",
    )(ctrl, pool)


def pack_share(wide, cores, head, ctrl, buffers):
    any_spec = pl.BlockSpec(memory_space=pl.ANY)
    return pl.pallas_call(
        lambda *refs: share_kernel(wide, cores, head * PAIR, *refs),
        out_shape=pages_shape(PMAX),
        grid_spec=pltpu.PrefetchScalarGridSpec(
            num_scalar_prefetch=1,
            grid=(1,),
            in_specs=[any_spec] * len(buffers),
            out_specs=any_spec,
            scratch_shapes=[pltpu.SemaphoreType.DMA((PMAX,))],
        ),
        compiler_params=params(),
        cost_estimate=pl.CostEstimate(
            flops=0, bytes_accessed=2 * 8 * BLOCK * PAIR * 2, transcendentals=0
        ),
        name=f"pack_share_{head}",
    )(ctrl, *buffers)


def fetch_pages(wide, cores, head, ctrl, pool):
    def hop(x, moves):
        pairs = [(a * cores + c, b * cores + c) for a, b in moves for c in range(cores)]
        return lax.ppermute(x, "wide", pairs)

    right, left, far = pack_send(wide, cores, head, ctrl, pool)
    from_left = hop(right, [(0, 1), (1, 2), (2, 3)])
    from_right = hop(left, [(3, 2), (2, 1), (1, 0)])
    from_far = hop(far, [(0, 2), (3, 1)])
    rows = FAR * BLOCK
    ahead = jnp.where(ctrl[ME_AT] // cores == 2, from_left[:rows], from_right[:rows])
    relayed = hop(jnp.concatenate([from_far[:rows], ahead], axis=0), [(2, 3), (1, 0)])
    buffers = [pool, from_left, from_right, from_far, relayed]
    shared = pack_share(wide, cores, head, ctrl, buffers)
    swap = [(d, d // cores * cores + (cores - 1 - d % cores)) for d in range(wide)]
    return buffers + [lax.ppermute(shared, "wide", swap)]


def project_kernel(at, *refs):
    parts, weight, out = refs[:-2], refs[-2], refs[-1]
    total = None
    for i, part in enumerate(parts):
        term = jnp.dot(
            part[...], weight[i * WIDTH : (i + 1) * WIDTH, :], preferred_element_type=jnp.float32
        )
        total = term if total is None else total + term
    out[...] = total.astype(jnp.bfloat16)


def project(parts, weight, first_column, columns):
    tokens = parts[0].shape[0]
    tile = math.gcd(columns, 512)
    at = jnp.reshape(first_column // tile, (1,)).astype(jnp.int32)
    return pl.pallas_call(
        project_kernel,
        out_shape=jax.ShapeDtypeStruct((tokens, columns), jnp.bfloat16),
        grid_spec=pltpu.PrefetchScalarGridSpec(
            num_scalar_prefetch=1,
            grid=(columns // tile,),
            in_specs=[pl.BlockSpec((tokens, WIDTH), lambda i, at: (0, 0))] * len(parts)
            + [pl.BlockSpec((weight.shape[0], tile), lambda i, at: (0, at[0] + i))],
            out_specs=pl.BlockSpec((tokens, tile), lambda i, at: (0, i)),
        ),
        compiler_params=params(),
        cost_estimate=pl.CostEstimate(
            flops=2 * tokens * columns * weight.shape[0],
            bytes_accessed=2 * columns * weight.shape[0],
            transcendentals=0,
        ),
        name="project",
    )(at, *parts, weight)


def local(
    queries, resp_kv, prefix_pool, out_weight, pre_len, prompt_blocks, prompt_owner, resp_seg
):
    wide, groups = lax.axis_size("wide"), lax.axis_size("tp") * lax.axis_size("sub")
    cores = 2 // lax.axis_size("sub")
    heads = resp_kv.shape[1] // PAIR
    me = lax.axis_index("wide").astype(jnp.int32)
    ctrl = jnp.concatenate([pre_len, prompt_blocks, prompt_owner, resp_seg, me[None]])
    if wide == 8 and cores == 2:
        buffers = [fetch_pages(wide, cores, g, ctrl, prefix_pool) for g in range(heads)]
    else:
        buffers = [[lax.all_gather(prefix_pool, "wide", axis=0, tiled=True)]] * heads
    parts = [
        attend(wide, cores, g, ctrl, queries, resp_kv, buffers[g]) for g in range(heads)
    ]
    columns = out_weight.shape[1]
    if groups != 2:
        terms = project(parts, out_weight, jnp.int32(0), columns)
        return lax.psum_scatter(terms, ("tp", "sub"), scatter_dimension=1, tiled=True)
    share = columns // groups
    group = lax.axis_index("tp") * lax.axis_size("sub") + lax.axis_index("sub")
    theirs = project(parts, out_weight, (1 - group) * share, share)
    axis = "tp" if lax.axis_size("tp") == 2 else "sub"
    arrived = lax.ppermute(theirs, axis, [(0, 1), (1, 0)])
    mine = project(parts, out_weight, group * share, share)
    return (mine.astype(jnp.float32) + arrived.astype(jnp.float32)).astype(jnp.bfloat16)


def solution(mesh):
    return jax.shard_map(
        local,
        mesh=mesh,
        in_specs=(
            P(("parts", "wide"), ("tp", "sub")),
            P(("parts", "wide"), ("tp", "sub")),
            P(("parts", "wide"), ("tp", "sub")),
            P(("tp", "sub"), None),
            P("parts"),
            P("parts"),
            P("parts"),
            P(("parts", "wide")),
        ),
        out_specs=P(("parts", "wide"), ("tp", "sub")),
        check_vma=False,
    )
```

time: 742 us -> 200 us (0.27)
  the two profiles are of different devices: /device:TPU:0 before, /device:TPU:6 now
where the time goes in v1:
time: 200 us; the launch traced here: 199 us
  Pallas kernels  85.2 us (43%)
  starting transfers between devices  55.6 us (28%)
  waiting for transfers between devices  41 us (20%)
  local copies, waits for them, and re-layouts  11.7 us (6%)
  other arithmetic  4.94 us (2%)
    ppermute x16, starting transfers between devices, hop(): return lax.ppermute(x, 'wide', pairs)  54.7 us
    pallas_call x4, Pallas kernels, attend(): pl.pallas_call(lambda *refs: attend_kernel(wide, cores, head * PAIR, *ref...  46.9 us
    pallas_call x2, Pallas kernels, project(): pl.pallas_call(project_kernel, out_shape=jax.ShapeDtypeStruct((tokens, co...  20.9 us
    ppermute x16, waiting for transfers between devices, hop(): return lax.ppermute(x, 'wide', pairs)  20.5 us
    ppermute x1, waiting for transfers between devices, local(): arrived = lax.ppermute(theirs, axis, [(0, 1), (1, 0)])  20.5 us
    pallas_call x4, Pallas kernels, pack_share(): pl.pallas_call(lambda *refs: share_kernel(wide, cores, head * PAIR, *refs...  11.8 us
    unnamed x74, local copies, waits for them, and re-layouts  10.9 us
    pallas_call x4, Pallas kernels, pack_send(): pl.pallas_call(lambda *refs: send_kernel(wide, cores, head * PAIR, *refs)...  5.6 us
  transfers between devices with their start and end apart: 21, of which 5 were waited for; matrix products, arithmetic and copies ran while one was open for 1% of the time, Pallas kernels for 31%

profile of v1, /device:TPU:6, one launch (start us, length us, event | category | flops | bytes accessed | tf_op | source)
XLA Modules:
  0.0 199.3 jit_solution(10745417989402528601)
XLA Ops:
  0.8 1.6 copy-done
  2.4 1.6 pack_send_3.1
  4.0 3.6 %collective-permute-start.15 = (bf16[768,256]{1,0:T(8,128)(2,1)}, bf16[768,256]{1,0:T(8,128)(2,1)S(1)}, u32[]{:S(2)}, u32[]{:S(2)}) collective-permute-start(bf16[768,256]{1,0:T(8,128)(2,1)} %get-tuple-element.26), channel_id=1, source_target_pairs={{0,4},{2,6},{4,8},{6,10},{8,12},{10,14},{1,5},{3,7},{5,9},{7,11},{... | collective-permute-start | bytes 1179656 | tf_op jit(solution)/shard_map/ppermute | solution.py:386
  7.6 1.3 collective-permute-start.16
  8.9 5.6 %collective-permute-start.17 = (bf16[768,256]{1,0:T(8,128)(2,1)}, bf16[768,256]{1,0:T(8,128)(2,1)S(1)}, u32[]{:S(2)}, u32[]{:S(2)}) collective-permute-start(bf16[768,256]{1,0:T(8,128)(2,1)} %get-tuple-element.28), channel_id=1, source_target_pairs={{0,8},{2,10},{12,4},{14,6},{1,9},{3,11},{13,5},{15,7},{16,24},{18,... | collective-permute-start | bytes 1179656 | tf_op jit(solution)/shard_map/ppermute | solution.py:386
  14.5 1.5 pack_send_2.1
  16.0 2.1 %collective-permute-start.10 = (bf16[768,256]{1,0:T(8,128)(2,1)}, bf16[768,256]{1,0:T(8,128)(2,1)}, u32[]{:S(2)}, u32[]{:S(2)}) collective-permute-start(bf16[768,256]{1,0:T(8,128)(2,1)} %get-tuple-element.23), channel_id=1, source_target_pairs={{0,4},{2,6},{4,8},{6,10},{8,12},{10,14},{1,5},{3,7},{5,9},{7,11},{... | collective-permute-start | bytes 1179656 | tf_op jit(solution)/shard_map/ppermute | solution.py:386
  26.5 4.1 %collective-permute-start.12 = (bf16[768,256]{1,0:T(8,128)(2,1)}, bf16[768,256]{1,0:T(8,128)(2,1)S(1)}, u32[]{:S(2)}, u32[]{:S(2)}) collective-permute-start(bf16[768,256]{1,0:T(8,128)(2,1)} %copy-done.34), channel_id=1, source_target_pairs={{0,8},{2,10},{12,4},{14,6},{1,9},{3,11},{13,5},{15,7},{16,24},{18,... | collective-permute-start | bytes 1179656 | tf_op jit(solution)/shard_map/ppermute | solution.py:386
  30.6 1.9 collective-permute-start.5
  32.5 1.3 collective-permute-start.6
  34.9 12.2 %collective-permute-start.7 = (bf16[768,256]{1,0:T(8,128)(2,1)S(1)}, bf16[768,256]{1,0:T(8,128)(2,1)S(1)}, u32[]{:S(2)}, u32[]{:S(2)}) collective-permute-start(bf16[768,256]{1,0:T(8,128)(2,1)S(1)} %copy-done.33), channel_id=1, source_target_pairs={{0,8},{2,10},{12,4},{14,6},{1,9},{3,11},{13,5},{15,7},{16,24},{18,... | collective-permute-start | bytes 1179656 | tf_op jit(solution)/shard_map/ppermute | solution.py:386
  47.1 1.3 collective-permute-start.18
  49.5 4.6 %collective-permute-start = (bf16[768,256]{1,0:T(8,128)(2,1)S(1)}, bf16[768,256]{1,0:T(8,128)(2,1)S(1)}, u32[]{:S(2)}, u32[]{:S(2)}) collective-permute-start(bf16[768,256]{1,0:T(8,128)(2,1)S(1)} %copy-done.31), channel_id=1, source_target_pairs={{0,4},{2,6},{4,8},{6,10},{8,12},{10,14},{1,5},{3,7},{5,9},{7,11},{... | collective-permute-start | bytes 1179656 | tf_op jit(solution)/shard_map/ppermute | solution.py:386
  55.4 10.3 %collective-permute-start.2 = (bf16[768,256]{1,0:T(8,128)(2,1)S(1)}, bf16[768,256]{1,0:T(8,128)(2,1)S(1)}, u32[]{:S(2)}, u32[]{:S(2)}) collective-permute-start(bf16[768,256]{1,0:T(8,128)(2,1)S(1)} %copy-done.27), channel_id=1, source_target_pairs={{0,8},{2,10},{12,4},{14,6},{1,9},{3,11},{13,5},{15,7},{16,24},{18,... | collective-permute-start | bytes 1179656 | tf_op jit(solution)/shard_map/ppermute | solution.py:386
  65.8 1.4 collective-permute-start.13
  68.7 4.1 %pack_share_3.1 = bf16[2048,256]{1,0:T(8,128)(2,1)} custom-call(s32[15]{0:T(128)S(1)} %concatenate.15.refs_0_, bf16[1024,1024]{1,0:T(8,128)(2,1)S(1)} %copy-done.1, bf16[768,256]{1,0:T(8,128)(2,1)S(1)} %copy-done.5, bf16[768,256]{1,0:T(8,128)(2,1)} %collective-permute-done.16.refs_3_.refs_5_, bf16[768,256]{1,0:T(8,128)(2,1)S(1)} %collective-permute-done.17.refs_4_.refs_6_, ...), custom_call_target="tpu_custom_call" | custom-call | bytes 1048576 | tf_op jit(solution)/shard_map/pack_share_3/pallas_call | solution.py:365
  72.9 2.3 %collective-permute-done.2.refs_4_.refs_6_ = bf16[768,256]{1,0:T(8,128)(2,1)S(1)} collective-permute-done((bf16[768,256]{1,0:T(8,128)(2,1)S(1)}, bf16[768,256]{1,0:T(8,128)(2,1)S(1)}, u32[]{:S(2)}, u32[]{:S(2)}) %collective-permute-start.2) | collective-permute-done | bytes 393248 | tf_op jit(solution)/shard_map/ppermute | solution.py:386
  76.6 6.1 %collective-permute-done.13.refs_5_.refs_7_ = bf16[1024,256]{1,0:T(8,128)(2,1)S(1)} collective-permute-done((bf16[1024,256]{1,0:T(8,128)(2,1)S(1)}, bf16[1024,256]{1,0:T(8,128)(2,1)S(1)}, u32[]{:S(2)}, u32[]{:S(2)}) %collective-permute-start.13) | collective-permute-done | bytes 524320 | tf_op jit(solution)/shard_map/ppermute | solution.py:386
  82.7 4.1 %pack_share_2.1 = bf16[2048,256]{1,0:T(8,128)(2,1)} custom-call(s32[15]{0:T(128)S(1)} %concatenate.15.refs_0_, bf16[1024,1024]{1,0:T(8,128)(2,1)S(1)} %copy-done.1, bf16[768,256]{1,0:T(8,128)(2,1)} %collective-permute-done.10.refs_2_.refs_4_, bf16[768,256]{1,0:T(8,128)(2,1)} %collective-permute-done.11.refs_3_.refs_5_, ...), custom_call_target="tpu_custom_call" | custom-call | bytes 1048576 | tf_op jit(solution)/shard_map/pack_share_2/pallas_call | solution.py:365
  86.9 7.0 %collective-permute-done.8.refs_5_.refs_7_ = bf16[1024,256]{1,0:T(8,128)(2,1)S(1)} collective-permute-done((bf16[1024,256]{1,0:T(8,128)(2,1)S(1)}, bf16[1024,256]{1,0:T(8,128)(2,1)S(1)}, u32[]{:S(2)}, u32[]{:S(2)}) %collective-permute-start.8) | collective-permute-done | bytes 524320 | tf_op jit(solution)/shard_map/ppermute | solution.py:386
  94.0 1.8 pack_share_1.1
  95.9 5.0 %collective-permute-done.3.refs_5_.refs_7_ = bf16[1024,256]{1,0:T(8,128)(2,1)S(1)} collective-permute-done((bf16[1024,256]{1,0:T(8,128)(2,1)S(1)}, bf16[1024,256]{1,0:T(8,128)(2,1)S(1)}, u32[]{:S(2)}, u32[]{:S(2)}) %collective-permute-start.3) | collective-permute-done | bytes 524320 | tf_op jit(solution)/shard_map/ppermute | solution.py:386
  100.9 1.8 pack_share_0.1
  104.9 1.6 copy-done.23
  107.5 11.5 %attend_head_3.1.refs_3_ = bf16[256,1024]{1,0:T(8,128)(2,1)S(1)} custom-call(s32[15]{0:T(128)S(1)} %concatenate.15.refs_0_, bf16[256,4096]{1,0:T(8,128)(2,1)S(1)} %copy-done.23, bf16[256,1024]{1,0:T(8,128)(2,1)S(1)} %copy-done.24, bf16[1024,1024]{1,0:T(8,128)(2,1)} %refs_3_.7, bf16[768,256]{1,0:T(8,128)(2,1)S(1)} %copy-done.6, ...), custom_call_target="tpu_custom_call" | custom-call | flops 2415919104 | bytes 2097152 | tf_op jit(solution)/shard_map/attend_head_3/pallas_call | solution.py:309
  119.1 11.8 %attend_head_2.1.refs_2_ = bf16[256,1024]{1,0:T(8,128)(2,1)S(1)} custom-call(s32[15]{0:T(128)S(1)} %concatenate.15.refs_0_, bf16[256,4096]{1,0:T(8,128)(2,1)S(1)} %copy-done.23, bf16[256,1024]{1,0:T(8,128)(2,1)S(1)} %copy-done.25, bf16[1024,1024]{1,0:T(8,128)(2,1)} %refs_3_.7, bf16[768,256]{1,0:T(8,128)(2,1)} %collective-permute-done.10.refs_2_.refs_4_, ...), custom_call_target="tpu_custom_call" | custom-call | flops 2415919104 | bytes 2097152 | tf_op jit(solution)/shard_map/attend_head_2/pallas_call | solution.py:309
  131.0 11.7 %attend_head_1.1.refs_1_ = bf16[256,1024]{1,0:T(8,128)(2,1)S(1)} custom-call(s32[15]{0:T(128)S(1)} %concatenate.15.refs_0_, bf16[256,4096]{1,0:T(8,128)(2,1)S(1)} %copy-done.23, bf16[256,1024]{1,0:T(8,128)(2,1)S(1)} %copy-done.25, bf16[1024,1024]{1,0:T(8,128)(2,1)} %refs_3_.7, bf16[768,256]{1,0:T(8,128)(2,1)S(1)} %copy-done.8, ...), custom_call_target="tpu_custom_call" | custom-call | flops 2415919104 | bytes 2097152 | tf_op jit(solution)/shard_map/attend_head_1/pallas_call | solution.py:309
  142.8 11.9 %attend_head_0.1.refs_0_ = bf16[256,1024]{1,0:T(8,128)(2,1)S(1)} custom-call(s32[15]{0:T(128)S(1)} %concatenate.15.refs_0_, bf16[256,4096]{1,0:T(8,128)(2,1)S(1)} %copy-done.23, bf16[256,1024]{1,0:T(8,128)(2,1)S(1)} %copy-done.25, bf16[1024,1024]{1,0:T(8,128)(2,1)} %refs_3_.7, bf16[768,256]{1,0:T(8,128)(2,1)S(1)} %copy-done.12, ...), custom_call_target="tpu_custom_call" | custom-call | flops 2415919104 | bytes 2097152 | tf_op jit(solution)/shard_map/attend_head_0/pallas_call | solution.py:309
  154.7 10.4 %project.3 = bf16[256,2560]{1,0:T(8,128)(2,1)S(1)} custom-call(s32[1]{0:T(128)} %bitcast.2.at, bf16[256,1024]{1,0:T(8,128)(2,1)S(1)} %attend_head_0.1.refs_0_, bf16[256,1024]{1,0:T(8,128)(2,1)S(1)} %attend_head_1.1.refs_1_, bf16[256,1024]{1,0:T(8,128)(2,1)S(1)} %attend_head_2.1.refs_2_, bf16[256,1024]{1,0:T(8,128)(2,1)S(1)} %attend_head_3.1.refs_3_, ...), custom_call_target="tpu_custom_call" | custom-call | flops 5368709120 | bytes 20971520 | tf_op jit(solution)/shard_map/project/pallas_call | solution.py:416
  165.7 10.4 %project.2 = bf16[256,2560]{1,0:T(8,128)(2,1)S(1)} custom-call(s32[1]{0:T(128)} %bitcast.at, bf16[256,1024]{1,0:T(8,128)(2,1)S(1)} %attend_head_0.1.refs_0_, bf16[256,1024]{1,0:T(8,128)(2,1)S(1)} %attend_head_1.1.refs_1_, bf16[256,1024]{1,0:T(8,128)(2,1)S(1)} %attend_head_2.1.refs_2_, bf16[256,1024]{1,0:T(8,128)(2,1)S(1)} %attend_head_3.1.refs_3_, ...), custom_call_target="tpu_custom_call" | custom-call | flops 5368709120 | bytes 20971520 | tf_op jit(solution)/shard_map/project/pallas_call | solution.py:416
  176.1 20.5 %collective-permute-done.20 = bf16[256,2560]{1,0:T(8,128)(2,1)} collective-permute-done((bf16[256,2560]{1,0:T(8,128)(2,1)S(1)}, bf16[256,2560]{1,0:T(8,128)(2,1)}, u32[]{:S(2)}, u32[]{:S(2)}) %collective-permute-start.20) | collective-permute-done | bytes 1310752 | tf_op jit(solution)/shard_map/ppermute | solution.py:459
  196.6 2.7 %add_convert_fusion = bf16[256,2560]{1,0:T(8,128)(2,1)} fusion(bf16[256,2560]{1,0:T(8,128)(2,1)} %collective-permute-done.20, bf16[256,2560]{1,0:T(8,128)(2,1)S(1)} %project.2), kind=kLoop, calls=%fused_computation | loop fusion | flops 2621440 | bytes 3932160 | tf_op jit(solution)/shard_map/convert_element_type | solution.py:461
  (112 shorter events, 19.4 us)
Async XLA Ops:
  3.9 15.5 %copy-start.1 = (bf16[1024,1024]{1,0:T(8,128)(2,1)S(1)}, bf16[1024,1024]{1,0:T(8,128)(2,1)}, u32[]{:S(2)}) copy-start(bf16[1024,1024]{1,0:T(8,128)(2,1)} %refs_3_.7) | copy-start | bytes 6291460
  4.0 22.5 %collective-permute-start.15 = (bf16[768,256]{1,0:T(8,128)(2,1)}, bf16[768,256]{1,0:T(8,128)(2,1)S(1)}, u32[]{:S(2)}, u32[]{:S(2)}) collective-permute-start(bf16[768,256]{1,0:T(8,128)(2,1)} %get-tuple-element.26), channel_id=1, source_target_pairs={{0,4},{2,6},{4,8},{6,10},{8,12},{10,14},{1,5},{3,7},{5,9},{7,11},{... | collective-permute-start | bytes 1179656 | tf_op jit(solution)/shard_map/ppermute | solution.py:386
  7.6 23.0 %collective-permute-start.16 = (bf16[768,256]{1,0:T(8,128)(2,1)}, bf16[768,256]{1,0:T(8,128)(2,1)}, u32[]{:S(2)}, u32[]{:S(2)}) collective-permute-start(bf16[768,256]{1,0:T(8,128)(2,1)} %get-tuple-element.27), channel_id=1, source_target_pairs={{12,8},{14,10},{8,4},{10,6},{4,0},{6,2},{13,9},{15,11},{9,5},{11,7... | collective-permute-start | bytes 1179656 | tf_op jit(solution)/shard_map/ppermute | solution.py:386
  8.9 23.6 %collective-permute-start.17 = (bf16[768,256]{1,0:T(8,128)(2,1)}, bf16[768,256]{1,0:T(8,128)(2,1)S(1)}, u32[]{:S(2)}, u32[]{:S(2)}) collective-permute-start(bf16[768,256]{1,0:T(8,128)(2,1)} %get-tuple-element.28), channel_id=1, source_target_pairs={{0,8},{2,10},{12,4},{14,6},{1,9},{3,11},{13,5},{15,7},{16,24},{18,... | collective-permute-start | bytes 1179656 | tf_op jit(solution)/shard_map/ppermute | solution.py:386
  16.0 18.8 %collective-permute-start.10 = (bf16[768,256]{1,0:T(8,128)(2,1)}, bf16[768,256]{1,0:T(8,128)(2,1)}, u32[]{:S(2)}, u32[]{:S(2)}) collective-permute-start(bf16[768,256]{1,0:T(8,128)(2,1)} %get-tuple-element.23), channel_id=1, source_target_pairs={{0,4},{2,6},{4,8},{6,10},{8,12},{10,14},{1,5},{3,7},{5,9},{7,11},{... | collective-permute-start | bytes 1179656 | tf_op jit(solution)/shard_map/ppermute | solution.py:386
  18.1 29.0 %collective-permute-start.11 = (bf16[768,256]{1,0:T(8,128)(2,1)}, bf16[768,256]{1,0:T(8,128)(2,1)}, u32[]{:S(2)}, u32[]{:S(2)}) collective-permute-start(bf16[768,256]{1,0:T(8,128)(2,1)} %get-tuple-element.24), channel_id=1, source_target_pairs={{12,8},{14,10},{8,4},{10,6},{4,0},{6,2},{13,9},{15,11},{9,5},{11,7... | collective-permute-start | bytes 1179656 | tf_op jit(solution)/shard_map/ppermute | solution.py:386
  26.5 23.0 %collective-permute-start.12 = (bf16[768,256]{1,0:T(8,128)(2,1)}, bf16[768,256]{1,0:T(8,128)(2,1)S(1)}, u32[]{:S(2)}, u32[]{:S(2)}) collective-permute-start(bf16[768,256]{1,0:T(8,128)(2,1)} %copy-done.34), channel_id=1, source_target_pairs={{0,8},{2,10},{12,4},{14,6},{1,9},{3,11},{13,5},{15,7},{16,24},{18,... | collective-permute-start | bytes 1179656 | tf_op jit(solution)/shard_map/ppermute | solution.py:386
  30.6 23.5 %collective-permute-start.5 = (bf16[768,256]{1,0:T(8,128)(2,1)}, bf16[768,256]{1,0:T(8,128)(2,1)S(1)}, u32[]{:S(2)}, u32[]{:S(2)}) collective-permute-start(bf16[768,256]{1,0:T(8,128)(2,1)} %copy-done.36), channel_id=1, source_target_pairs={{0,4},{2,6},{4,8},{6,10},{8,12},{10,14},{1,5},{3,7},{5,9},{7,11},{... | collective-permute-start | bytes 1179656 | tf_op jit(solution)/shard_map/ppermute | solution.py:386
  32.5 22.9 %collective-permute-start.6 = (bf16[768,256]{1,0:T(8,128)(2,1)}, bf16[768,256]{1,0:T(8,128)(2,1)S(1)}, u32[]{:S(2)}, u32[]{:S(2)}) collective-permute-start(bf16[768,256]{1,0:T(8,128)(2,1)} %copy-done.35), channel_id=1, source_target_pairs={{12,8},{14,10},{8,4},{10,6},{4,0},{6,2},{13,9},{15,11},{9,5},{11,7... | collective-permute-start | bytes 1179656 | tf_op jit(solution)/shard_map/ppermute | solution.py:386
  34.8 14.7 %copy-start.31 = (bf16[768,256]{1,0:T(8,128)(2,1)S(1)}, bf16[768,256]{1,0:T(8,128)(2,1)}, u32[]{:S(2)}) copy-start(bf16[768,256]{1,0:T(8,128)(2,1)} %copy-done.30) | copy-start | bytes 1179652
  34.8 19.3 %copy-start.29 = (bf16[768,256]{1,0:T(8,128)(2,1)S(1)}, bf16[768,256]{1,0:T(8,128)(2,1)}, u32[]{:S(2)}) copy-start(bf16[768,256]{1,0:T(8,128)(2,1)} %copy-done.28) | copy-start | bytes 1179652
  34.8 20.6 %copy-start.27 = (bf16[768,256]{1,0:T(8,128)(2,1)S(1)}, bf16[768,256]{1,0:T(8,128)(2,1)}, u32[]{:S(2)}) copy-start(bf16[768,256]{1,0:T(8,128)(2,1)} %copy-done.26) | copy-start | bytes 1179652
  34.9 30.9 %collective-permute-start.7 = (bf16[768,256]{1,0:T(8,128)(2,1)S(1)}, bf16[768,256]{1,0:T(8,128)(2,1)S(1)}, u32[]{:S(2)}, u32[]{:S(2)}) collective-permute-start(bf16[768,256]{1,0:T(8,128)(2,1)S(1)} %copy-done.33), channel_id=1, source_target_pairs={{0,8},{2,10},{12,4},{14,6},{1,9},{3,11},{13,5},{15,7},{16,24},{18,... | collective-permute-start | bytes 1179656 | tf_op jit(solution)/shard_map/ppermute | solution.py:386
  47.1 20.3 %collective-permute-start.18 = (bf16[1024,256]{1,0:T(8,128)(2,1)S(1)}, bf16[1024,256]{1,0:T(8,128)(2,1)S(1)}, u32[]{:S(2)}, u32[]{:S(2)}) collective-permute-start(bf16[1024,256]{1,0:T(8,128)(2,1)S(1)} %pad_maximum_fusion.3), channel_id=1, source_target_pairs={{8,12},{10,14},{4,0},{6,2},{9,13},{11,15},{5,1},{7,3},{24,28},{26,... | collective-permute-start | bytes 1572872 | tf_op jit(solution)/shard_map/ppermute | solution.py:386
  49.5 23.3 %collective-permute-start = (bf16[768,256]{1,0:T(8,128)(2,1)S(1)}, bf16[768,256]{1,0:T(8,128)(2,1)S(1)}, u32[]{:S(2)}, u32[]{:S(2)}) collective-permute-start(bf16[768,256]{1,0:T(8,128)(2,1)S(1)} %copy-done.31), channel_id=1, source_target_pairs={{0,4},{2,6},{4,8},{6,10},{8,12},{10,14},{1,5},{3,7},{5,9},{7,11},{... | collective-permute-start | bytes 1179656 | tf_op jit(solution)/shard_map/ppermute | solution.py:386
  54.1 39.9 %copy-start.7 = (bf16[768,256]{1,0:T(8,128)(2,1)}, bf16[768,256]{1,0:T(8,128)(2,1)S(1)}, u32[]{:S(2)}) copy-start(bf16[768,256]{1,0:T(8,128)(2,1)S(1)} %collective-permute-done.5.refs_2_.refs_4_) | copy-start | bytes 1179652
  54.1 18.8 %collective-permute-start.1 = (bf16[768,256]{1,0:T(8,128)(2,1)S(1)}, bf16[768,256]{1,0:T(8,128)(2,1)S(1)}, u32[]{:S(2)}, u32[]{:S(2)}) collective-permute-start(bf16[768,256]{1,0:T(8,128)(2,1)S(1)} %copy-done.29), channel_id=1, source_target_pairs={{12,8},{14,10},{8,4},{10,6},{4,0},{6,2},{13,9},{15,11},{9,5},{11,7... | collective-permute-start | bytes 1179656 | tf_op jit(solution)/shard_map/ppermute | solution.py:386
  55.4 38.5 %copy-start.9 = (bf16[768,256]{1,0:T(8,128)(2,1)}, bf16[768,256]{1,0:T(8,128)(2,1)S(1)}, u32[]{:S(2)}) copy-start(bf16[768,256]{1,0:T(8,128)(2,1)S(1)} %collective-permute-done.6.refs_3_.refs_5_) | copy-start | bytes 1179652
  55.4 19.8 %collective-permute-start.2 = (bf16[768,256]{1,0:T(8,128)(2,1)S(1)}, bf16[768,256]{1,0:T(8,128)(2,1)S(1)}, u32[]{:S(2)}, u32[]{:S(2)}) collective-permute-start(bf16[768,256]{1,0:T(8,128)(2,1)S(1)} %copy-done.27), channel_id=1, source_target_pairs={{0,8},{2,10},{12,4},{14,6},{1,9},{3,11},{13,5},{15,7},{16,24},{18,... | collective-permute-start | bytes 1179656 | tf_op jit(solution)/shard_map/ppermute | solution.py:386
  65.8 16.9 %collective-permute-start.13 = (bf16[1024,256]{1,0:T(8,128)(2,1)S(1)}, bf16[1024,256]{1,0:T(8,128)(2,1)S(1)}, u32[]{:S(2)}, u32[]{:S(2)}) collective-permute-start(bf16[1024,256]{1,0:T(8,128)(2,1)S(1)} %pad_maximum_fusion.2), channel_id=1, source_target_pairs={{8,12},{10,14},{4,0},{6,2},{9,13},{11,15},{5,1},{7,3},{24,28},{26,... | collective-permute-start | bytes 1572872 | tf_op jit(solution)/shard_map/ppermute | solution.py:386
  67.3 26.6 %collective-permute-start.8 = (bf16[1024,256]{1,0:T(8,128)(2,1)S(1)}, bf16[1024,256]{1,0:T(8,128)(2,1)S(1)}, u32[]{:S(2)}, u32[]{:S(2)}) collective-permute-start(bf16[1024,256]{1,0:T(8,128)(2,1)S(1)} %pad_maximum_fusion.1), channel_id=1, source_target_pairs={{8,12},{10,14},{4,0},{6,2},{9,13},{11,15},{5,1},{7,3},{24,28},{26,... | collective-permute-start | bytes 1572872 | tf_op jit(solution)/shard_map/ppermute | solution.py:386
  72.8 28.1 %copy-start.11 = (bf16[768,256]{1,0:T(8,128)(2,1)}, bf16[768,256]{1,0:T(8,128)(2,1)S(1)}, u32[]{:S(2)}) copy-start(bf16[768,256]{1,0:T(8,128)(2,1)S(1)} %collective-permute-done.refs_2_.refs_4_) | copy-start | bytes 1179652
  72.8 30.0 %collective-permute-start.19 = (bf16[2048,256]{1,0:T(8,128)(2,1)}, bf16[2048,256]{1,0:T(8,128)(2,1)}, u32[]{:S(2)}, u32[]{:S(2)}) collective-permute-start(bf16[2048,256]{1,0:T(8,128)(2,1)} %pack_share_3.1), channel_id=1, source_target_pairs={{0,2},{2,0},{4,6},{6,4},{8,10},{10,8},{12,14},{14,12},{1,3},{3,1},... | collective-permute-start | bytes 3145736 | tf_op jit(solution)/shard_map/ppermute | solution.py:398
  72.9 28.0 %copy-start.13 = (bf16[768,256]{1,0:T(8,128)(2,1)}, bf16[768,256]{1,0:T(8,128)(2,1)S(1)}, u32[]{:S(2)}) copy-start(bf16[768,256]{1,0:T(8,128)(2,1)S(1)} %collective-permute-done.1.refs_3_.refs_5_) | copy-start | bytes 1179652
  75.3 25.6 %copy-start.2 = (bf16[768,256]{1,0:T(8,128)(2,1)}, bf16[768,256]{1,0:T(8,128)(2,1)S(1)}, u32[]{:S(2)}) copy-start(bf16[768,256]{1,0:T(8,128)(2,1)S(1)} %collective-permute-done.2.refs_4_.refs_6_) | copy-start | bytes 1179652
  75.3 25.5 %collective-permute-start.3 = (bf16[1024,256]{1,0:T(8,128)(2,1)S(1)}, bf16[1024,256]{1,0:T(8,128)(2,1)S(1)}, u32[]{:S(2)}, u32[]{:S(2)}) collective-permute-start(bf16[1024,256]{1,0:T(8,128)(2,1)S(1)} %pad_maximum_fusion), channel_id=1, source_target_pairs={{8,12},{10,14},{4,0},{6,2},{9,13},{11,15},{5,1},{7,3},{24,28},{26,... | collective-permute-start | bytes 1572872 | tf_op jit(solution)/shard_map/ppermute | solution.py:386
  86.8 32.3 %collective-permute-start.14 = (bf16[2048,256]{1,0:T(8,128)(2,1)}, bf16[2048,256]{1,0:T(8,128)(2,1)}, u32[]{:S(2)}, u32[]{:S(2)}) collective-permute-start(bf16[2048,256]{1,0:T(8,128)(2,1)} %pack_share_2.1), channel_id=1, source_target_pairs={{0,2},{2,0},{4,6},{6,4},{8,10},{10,8},{12,14},{14,12},{1,3},{3,1},... | collective-permute-start | bytes 3145736 | tf_op jit(solution)/shard_map/ppermute | solution.py:398
  95.8 35.2 %collective-permute-start.9 = (bf16[2048,256]{1,0:T(8,128)(2,1)}, bf16[2048,256]{1,0:T(8,128)(2,1)}, u32[]{:S(2)}, u32[]{:S(2)}) collective-permute-start(bf16[2048,256]{1,0:T(8,128)(2,1)} %pack_share_1.1), channel_id=1, source_target_pairs={{0,2},{2,0},{4,6},{6,4},{8,10},{10,8},{12,14},{14,12},{1,3},{3,1},... | collective-permute-start | bytes 3145736 | tf_op jit(solution)/shard_map/ppermute | solution.py:398
  102.7 40.0 %collective-permute-start.4 = (bf16[2048,256]{1,0:T(8,128)(2,1)}, bf16[2048,256]{1,0:T(8,128)(2,1)}, u32[]{:S(2)}, u32[]{:S(2)}) collective-permute-start(bf16[2048,256]{1,0:T(8,128)(2,1)} %pack_share_0.1), channel_id=1, source_target_pairs={{0,2},{2,0},{4,6},{6,4},{8,10},{10,8},{12,14},{14,12},{1,3},{3,1},... | collective-permute-start | bytes 3145736 | tf_op jit(solution)/shard_map/ppermute | solution.py:398
  119.1 11.9 %copy-start.8 = (bf16[768,256]{1,0:T(8,128)(2,1)S(1)}, bf16[768,256]{1,0:T(8,128)(2,1)}, u32[]{:S(2)}) copy-start(bf16[768,256]{1,0:T(8,128)(2,1)} %copy-done.7) | copy-start | bytes 1179652
  119.1 11.9 %copy-start.10 = (bf16[768,256]{1,0:T(8,128)(2,1)S(1)}, bf16[768,256]{1,0:T(8,128)(2,1)}, u32[]{:S(2)}) copy-start(bf16[768,256]{1,0:T(8,128)(2,1)} %copy-done.9) | copy-start | bytes 1179652
  165.1 31.5 %collective-permute-start.20 = (bf16[256,2560]{1,0:T(8,128)(2,1)S(1)}, bf16[256,2560]{1,0:T(8,128)(2,1)}, u32[]{:S(2)}, u32[]{:S(2)}) collective-permute-start(bf16[256,2560]{1,0:T(8,128)(2,1)S(1)} %project.3), channel_id=1, source_target_pairs={{0,1},{1,0},{2,3},{3,2},{4,5},{5,4},{6,7},{7,6},{8,9},{9,8},{10,11... | collective-permute-start | bytes 3932168 | tf_op jit(solution)/shard_map/ppermute | solution.py:459
  (26 other events, 129.4 us)
